TPU v7x, 512 devices: a whole 4x4x16 slice. The times are simulated.
512 devices in a mesh: row: 16 (over z), col: 32 (over y, x, core).
Axes of the slice: x: 4, y: 4, z: 16, core: 2. Of those that a mesh axis runs over, the one named last changes fastest.
Arguments:
- x_panel: bfloat16 [8192, 4096], P('col', 'row'), may hold values from -16 to 16
- grad_out: bfloat16 [2, 8192, 10240], P(None, 'row', 'col'), may hold values from -0.1 to 0.1
- row_state: float32 [2, 4096], P(None, 'row'), may hold values from 0 to 163.84, as said below
- col_state: float32 [2, 10240], P(None, 'col'), may hold values from 0 to 163.84, as said below
Outputs:
- direction: float32 [2, 4096, 10240], P(None, 'row', 'col')
- new_rows: float32 [2, 4096], P(None, 'row')
- new_cols: float32 [2, 10240], P(None, 'col')
Inputs may be any that keep to these rules, and one draw needn't show every extreme that they name: `row_state`: positive. `col_state`: positive.
All inputs are finite; a program needn't handle non-finite values.
Results may differ from a plain program's by a relative error of at most 0.0003.
Values may be sent and summed in bfloat16 or wider, within the bound.
A program may use at most 64 MiB of HBM per device.

v0:
```python
import jax
import jax.numpy as jnp
from jax import lax
from jax.sharding import PartitionSpec as P

D = 4096
FF = 10240


def shards(x_panel, grad_out, row_state, col_state):
    x_whole = lax.all_gather(x_panel, "col", axis=0, tiled=True)
    gradient = jnp.einsum(
        "tr,mtc->mrc",
        x_whole,
        lax.all_gather(grad_out, "row", axis=1, tiled=True),
        preferred_element_type=jnp.float32,
    )
    squares = gradient * gradient + 1e-30
    row_part = jnp.sum(squares, axis=2)
    col_part = jnp.sum(squares, axis=1)
    col_total = lax.psum(col_part, "row")
    new_cols = 0.7 * col_state + 0.3 * (col_total / D)
    row_total = lax.psum(row_part, "col")
    new_rows = 0.7 * row_state + 0.3 * (row_total / FF)
    row_level = lax.psum(jnp.sum(new_rows, axis=1), "row") / D
    update = gradient * lax.rsqrt(
        new_rows[:, :, None] * new_cols[:, None, :] / row_level[:, None, None]
    )
    update_total = lax.psum(jnp.sum(update * update, axis=(1, 2)), ("row", "col"))
    urms = jnp.sqrt(update_total / (D * FF))
    direction = update / jnp.maximum(1.0, urms)[:, None, None]
    return (direction, new_rows, new_cols)


def solution(mesh):
    return jax.shard_map(
        shards,
        mesh=mesh,
        in_specs=(P("col", "row"), P(None, "row", "col"), P(None, "row"), P(None, "col")),
        out_specs=(P(None, "row", "col"), P(None, "row"), P(None, "col")),
        check_vma=False,
    )
```

profile of v0, /device:TPU:1, one launch (start us, length us, event | category | flops | bytes accessed | tf_op | source)
XLA Modules:
  0.0 415.3 jit_solution(2371214969229405645)
XLA Ops:
  7.2 0.0 all-gather.5.cloned.1.call-start
  7.2 0.7 all-gather.5.cloned.1.call-update
  7.9 0.0 all-gather.3.cloned.1.call-start
  7.9 0.7 all-gather.3.cloned.1.call-update
  8.6 0.0 copy-start.3
  8.7 0.0 copy-start.2
  8.7 69.6 %all-gather.5.cloned.1.call-done = bf16[8192,256]{1,0:T(8,128)(2,1)} async-done(((bf16[256,256]{1,0:T(8,128)(2,1)}), bf16[8192,256]{1,0:T(8,128)(2,1)}) %all-gather.5.cloned.1.call-update) | async-done | bytes 4194320 | tf_op jit(solution)/shard_map/all_gather | solution.py:11
  78.3 128.2 %all-gather.3.cloned.1.call-done = bf16[2,8192,320]{1,2,0:T(8,128)(2,1)} async-done(((bf16[2,512,320]{1,2,0:T(8,128)(2,1)}), bf16[2,8192,320]{1,2,0:T(8,128)(2,1)}) %all-gather.3.cloned.1.call-update) | async-done | bytes 10485776 | tf_op jit(solution)/shard_map/all_gather | solution.py:15
  206.4 7.0 %fusion.5 = (f32[2,320]{1,0:T(2,128)S(1)}, f32[2,256]{1,0:T(2,128)S(1)}, f32[2,256,320]{1,2,0:T(8,128)S(1)}) fusion(bf16[2,8192,320]{1,2,0:T(8,128)(2,1)} %all-gather.3.cloned.1.call-done, bf16[8192,256]{1,0:T(8,128)(2,1)} %all-gather.5.cloned.1.call-done), kind=kOutput, calls=%fused_computation.6 | convolution fusion | flops 2685008896 | bytes 15340032 | tf_op jit(solution)/shard_map/tr,mtc->mrc/dot_general | solution.py:12
  213.4 62.7 %psum.28 = f32[2,256]{1,0:T(2,128)S(1)} all-reduce(f32[2,256]{1,0:T(2,128)S(1)} %get-tuple-element.4), channel_id=1, replica_groups=mesh['row'=16,'col'=32] {'col'}, use_global_device_ids=true, to_apply=%region_1.0 | all-reduce | flops 512 | bytes 4096 | tf_op jit(solution)/shard_map/psum | solution.py:23
  276.2 0.0 copy-done.3
  276.2 0.1 fusion.7
  276.3 0.0 copy-start.1
  276.3 21.7 %all-reduce = (f32[2]{0:T(128)S(1)}, f32[2,320]{1,0:T(2,128)S(1)}) all-reduce(f32[2]{0:T(128)S(1)} %get-tuple-element.7, f32[2,320]{1,0:T(2,128)S(1)} %get-tuple-element.3), channel_id=1, replica_groups=mesh['row'=16,'col'=32] {'row'}, use_global_device_ids=true, to_apply=%region_5.0 | all-reduce | flops 642 | bytes 5136 | tf_op jit(solution)/shard_map/psum | solution.py:25
  298.0 0.0 copy-done.2
  298.0 0.0 copy-start
  298.0 0.3 multiply_reduce_fusion
  298.3 109.0 %psum.31 = f32[2]{0:T(128)S(1)} all-reduce(f32[2]{0:T(128)S(1)} %multiply_reduce_fusion), channel_id=1, replica_groups=mesh['row'=16,'col'=32] {'row','col'}, use_global_device_ids=true, to_apply=%region_7.0 | all-reduce | flops 2 | bytes 16 | tf_op jit(solution)/shard_map/psum | solution.py:29
  407.4 1.0 broadcast_divide_fusion
  408.4 0.0 copy-done.1
  408.4 0.0 copy-done
  (3 shorter events, 0.0 us)
Async XLA Ops:
  7.2 71.1 %all-gather.5.cloned.1.call-start = ((), (), s32[]{:S(2)}) async-start(), calls=%async_computation.1 | async-start | bytes 4325376 | tf_op jit(solution)/shard_map/all_gather | solution.py:11
  7.9 198.5 %all-gather.3.cloned.1.call-start = ((), (), s32[]{:S(2)}) async-start(), calls=%async_computation | async-start | bytes 11141120 | tf_op jit(solution)/shard_map/all_gather | solution.py:15
  8.6 267.5 %copy-start.3 = (f32[2,256]{1,0:T(2,128)S(1)}, f32[2,256]{1,0:T(2,128)}, u32[]{:S(2)}) copy-start(f32[2,256]{1,0:T(2,128)} %param.6) | copy-start | bytes 6148
  8.7 289.3 %copy-start.2 = (f32[2,320]{1,0:T(2,128)S(1)}, f32[2,320]{1,0:T(2,128)}, u32[]{:S(2)}) copy-start(f32[2,320]{1,0:T(2,128)} %param.7) | copy-start | bytes 7684
  276.3 132.1 %copy-start.1 = (f32[2,256]{1,0:T(2,128)}, f32[2,256]{1,0:T(2,128)S(1)}, u32[]{:S(2)}) copy-start(f32[2,256]{1,0:T(2,128)S(1)} %get-tuple-element.8) | copy-start | bytes 6148
  298.0 110.4 %copy-start = (f32[2,320]{1,0:T(2,128)}, f32[2,320]{1,0:T(2,128)S(1)}, u32[]{:S(2)}) copy-start(f32[2,320]{1,0:T(2,128)S(1)} %multiply_add_fusion.1) | copy-start | bytes 7684
Sparse Core Ops, SparseCore 0:
  11.1 67.0 all-gather.4
  80.4 126.0 all-gather.2
where the time goes:
time: 415 us
  waiting for transfers between devices  199 us (48%)
  blocking collectives  193 us (47%)
  between operations  14.1 us (3%)
  matrix products  7 us (2%)
    all_gather x1, waiting for transfers between devices, shards(): lax.all_gather(grad_out, 'row', axis=1, tiled=True)  128 us
    psum x1, blocking collectives, shards(): lax.psum(jnp.sum(update * update, axis=(1, 2)), ('row', 'col'))  109 us
    all_gather x1, waiting for transfers between devices, shards(): x_whole = lax.all_gather(x_panel, 'col', axis=0, tiled=True)  69.6 us
    psum x1, blocking collectives, shards(): row_total = lax.psum(row_part, 'col')  62.7 us
    psum x1, blocking collectives, shards(): row_level = lax.psum(jnp.sum(new_rows, axis=1), 'row') / D  21.7 us
  transfers between devices with their start and end apart: 2, of which 2 were waited for; matrix products, arithmetic and copies ran while one was open for 0% of the time, Pallas kernels for 0%

commit v1 on v0

v1 whole, which is shorter than its diff:
```python
import jax
import jax.numpy as jnp
from jax import lax
from jax.experimental import pallas as pl
from jax.experimental.pallas import tpu as pltpu
from jax.sharding import PartitionSpec as P

D = 4096
FF = 10240
NZ = 16
NC = 32
TB = 512
XB = 256
FB = 256
HB = 320
W = 2 * HB
CH = 4
CT = TB // CH
START = 4

MESH = pl.DeviceIdType.MESH
f32 = jnp.float32


def kernel(
    x_hbm, g_hbm, rs_ref, cs_ref,
    grad_hbm, nr_ref, nc_ref, k_ref,
    gin, gbuf, xbuf, acc, split, rowx, colx, ux, s3x,
    lsem, grecv, gright, gleft, xrecv, xsend,
    rrecv, rsend, crecv, csend, urecv, usend, srecv, ssend,
):
    z = lax.axis_index("row")
    c = lax.axis_index("col")
    right = lax.rem(z + 1, NZ)
    left = lax.rem(z + NZ - 1, NZ)

    gcopy = [
        pltpu.make_async_copy(g_hbm.at[m], gin.at[m], lsem.at[m]) for m in range(2)
    ]
    xcopy = pltpu.make_async_copy(x_hbm, xbuf.at[c], lsem.at[2])
    for cp in gcopy:
        cp.start()
    xcopy.start()

    barrier = pltpu.get_barrier_semaphore()

    @pl.loop(1, NZ)
    def _(k):
        pl.semaphore_signal(
            barrier, inc=1, device_id=(lax.rem(z + k, NZ), c), device_id_type=MESH
        )

    @pl.loop(1, NC)
    def _(k):
        pl.semaphore_signal(
            barrier, inc=1, device_id=(z, lax.rem(c + k, NC)), device_id_type=MESH
        )

    pl.semaphore_wait(barrier, NZ - 1 + NC - 1)

    def piece(b, p):
        return gbuf.at[b, pl.ds(p * CT, CT), :]

    def hop(b, p, to_right):
        sems = gright if to_right else gleft
        return pltpu.make_async_remote_copy(
            src_ref=piece(b, p),
            dst_ref=piece(b, p),
            send_sem=sems.at[b, p],
            recv_sem=grecv.at[b, p],
            device_id=(right if to_right else left, c),
            device_id_type=MESH,
        )

    for cp in gcopy:
        cp.wait()
    for p in range(CH):
        rows = pl.ds(p * CT, CT)
        gbuf[z, rows, :] = jnp.concatenate([gin[0, rows, :], gin[1, rows, :]], axis=1)
        hop(z, p, True).start()
        hop(z, p, False).start()

    xcopy.wait()

    def xput(k):
        t = lax.rem(c + k, NC)
        return pltpu.make_async_remote_copy(
            src_ref=xbuf.at[c], dst_ref=xbuf.at[c],
            send_sem=xsend.at[k], recv_sem=xrecv.at[k],
            device_id=(z, t), device_id_type=MESH,
        )

    def xget(k):
        o = lax.rem(c + NC - k, NC)
        return pltpu.make_async_remote_copy(
            src_ref=xbuf.at[o], dst_ref=xbuf.at[o],
            send_sem=xsend.at[k], recv_sem=xrecv.at[k],
            device_id=(z, o), device_id_type=MESH,
        )

    @pl.loop(1, NC)
    def _(k):
        xput(k).start()

    acc[...] = jnp.zeros_like(acc)

    def mm(b):
        xa = jnp.concatenate([xbuf[2 * b], xbuf[2 * b + 1]], axis=0)
        acc[...] += lax.dot_general(
            xa, gbuf[b], (((0,), (0,)), ((), ())), preferred_element_type=f32
        )

    def mm_piece(b, p):
        per = XB // CT
        xa = xbuf[2 * b + p // per, pl.ds((p % per) * CT, CT), :]
        acc[...] += lax.dot_general(
            xa, gbuf[b, pl.ds(p * CT, CT), :], (((0,), (0,)), ((), ())),
            preferred_element_type=f32,
        )

    def from_left(s):
        return lax.rem(z + NZ - s, NZ)

    def from_right(s):
        return lax.rem(z + s, NZ)

    @pl.loop(1, START)
    def _(s):
        bl, br = from_left(s), from_right(s)
        for p in range(CH):
            hop(bl, p, True).wait_recv()
            hop(bl, p, True).start()
            hop(br, p, False).wait_recv()
            hop(br, p, False).start()

    @pl.loop(1, NC)
    def _(k):
        xget(k).wait_recv()

    @pl.loop(START, 7)
    def _(s):
        bl, br = from_left(s), from_right(s)
        q = 2 * (s - START)
        for p in range(CH):
            hop(bl, p, True).wait_recv()
            hop(bl, p, True).start()
            hop(br, p, False).wait_recv()
            hop(br, p, False).start()
            if p == 0:
                mm(from_left(q))
            elif p == 1:
                @pl.when(q > 0)
                def _():
                    mm(from_right(q))
            elif p == 2:
                mm(from_left(q + 1))
            elif p == 3:
                mm(from_right(q + 1))

    bl, br = from_left(7), from_right(7)
    for p in range(CH):
        hop(bl, p, True).wait_recv()
        if p < CH // 2:
            hop(bl, p, True).start()
        hop(br, p, False).wait_recv()
        if p >= CH // 2:
            hop(br, p, False).start()
        if p == 0:
            mm(from_left(6))
        elif p == 1:
            mm(from_right(6))
    mm(bl)
    mm(br)

    far = from_right(8)
    for p in range(CH // 2):
        for pp, to_right in ((p, True), (p + CH // 2, False)):
            hop(far, pp, to_right).wait_recv()
            mm_piece(far, pp)

    rsum = []
    for m in range(2):
        gm = acc[:, m * HB : (m + 1) * HB]
        split[m] = gm
        rsum.append(jnp.sum(gm * gm + 1e-30, axis=1, keepdims=True))
    lane = lax.broadcasted_iota(jnp.int32, (FB, 128), 1)
    rmat = jnp.where(lane == 0, rsum[0], rsum[1])
    rmat_t = rmat.T
    rowx[c, :, 0:FB] = rmat_t[0:1]
    rowx[c, :, FB : 2 * FB] = rmat_t[1:2]

    def put(buf, sends, recvs, k, along_row):
        if along_row:
            me, dev = z, (lax.rem(z + k, NZ), c)
        else:
            me, dev = c, (z, lax.rem(c + k, NC))
        return pltpu.make_async_remote_copy(
            src_ref=buf.at[me], dst_ref=buf.at[me],
            send_sem=sends.at[k], recv_sem=recvs.at[k],
            device_id=dev, device_id_type=MESH,
        )

    def get(buf, sends, recvs, k, along_row):
        if along_row:
            o = lax.rem(z + NZ - k, NZ)
            dev = (o, c)
        else:
            o = lax.rem(c + NC - k, NC)
            dev = (z, o)
        return pltpu.make_async_remote_copy(
            src_ref=buf.at[o], dst_ref=buf.at[o],
            send_sem=sends.at[k], recv_sem=recvs.at[k],
            device_id=dev, device_id_type=MESH,
        )

    def send_all(buf, sends, recvs, along_row):
        @pl.loop(1, NZ if along_row else NC)
        def _(k):
            put(buf, sends, recvs, k, along_row).start()

    def recv_all(buf, sends, recvs, along_row):
        @pl.loop(1, NZ if along_row else NC)
        def _(k):
            get(buf, sends, recvs, k, along_row).wait_recv()

    def drain(buf, sends, recvs, along_row):
        @pl.loop(1, NZ if along_row else NC)
        def _(k):
            put(buf, sends, recvs, k, along_row).wait_send()

    send_all(rowx, rsend, rrecv, False)

    out_copy = pltpu.make_async_copy(split, grad_hbm, lsem.at[3])
    out_copy.start()

    for m in range(2):
        gm = split[m]
        colx[z, :, m * 384 : m * 384 + HB] = jnp.sum(
            gm * gm + 1e-30, axis=0, keepdims=True
        )
    send_all(colx, csend, crecv, True)

    recv_all(rowx, rsend, rrecv, False)
    row_tot = jnp.sum(rowx[...], axis=0)
    nr = []
    for m in range(2):
        v = 0.7 * rs_ref[m : m + 1, :] + 0.3 * (row_tot[:, m * FB : (m + 1) * FB] / FF)
        nr_ref[m : m + 1, :] = v
        nr.append(v)
    sub = lax.broadcasted_iota(jnp.int32, (128, FB), 0)
    rcol = lax.rsqrt(jnp.where(sub == 0, nr[0], nr[1])).T
    lane1 = lax.broadcasted_iota(jnp.int32, (1, 128), 1)
    for m in range(2):
        u = split[m] * rcol[:, m : m + 1]
        ux[z, :, m * 384 : m * 384 + HB] = jnp.sum(u * u, axis=0, keepdims=True)
    level_part = jnp.where(
        lane1 == 0,
        jnp.sum(nr[0], axis=1, keepdims=True),
        jnp.sum(nr[1], axis=1, keepdims=True),
    )
    ux[z, :, 768:896] = level_part
    send_all(ux, usend, urecv, True)

    recv_all(colx, csend, crecv, True)
    col_tot = jnp.sum(colx[...], axis=0)
    nc = []
    for m in range(2):
        v = 0.7 * cs_ref[m : m + 1, :] + 0.3 * (col_tot[:, m * 384 : m * 384 + HB] / D)
        nc_ref[m : m + 1, :] = v
        nc.append(v)

    recv_all(ux, usend, urecv, True)
    u_tot = jnp.sum(ux[...], axis=0)
    s_part = [
        jnp.sum(u_tot[:, m * 384 : m * 384 + HB] / nc[m], axis=1, keepdims=True)
        for m in range(2)
    ]
    level = u_tot[:, 768:896] / D
    s3x[c] = jnp.where(lane1 == 0, s_part[0], s_part[1])
    send_all(s3x, ssend, srecv, False)
    recv_all(s3x, ssend, srecv, False)
    s_tot = jnp.sum(s3x[...], axis=0)
    urms = jnp.sqrt(level * (s_tot / (D * FF)))
    k_ref[...] = jnp.sqrt(level) / jnp.maximum(1.0, urms)

    drain(rowx, rsend, rrecv, False)
    drain(colx, csend, crecv, True)
    drain(ux, usend, urecv, True)
    drain(s3x, ssend, srecv, False)

    @pl.loop(1, NC)
    def _(k):
        xput(k).wait_send()

    @pl.loop(0, 7)
    def _(s):
        bl, br = from_left(s), from_right(s)
        for p in range(CH):
            hop(bl, p, True).wait_send()
            hop(br, p, False).wait_send()

    for p in range(CH // 2):
        hop(bl, p, True).wait_send()
        hop(br, p + CH // 2, False).wait_send()
    out_copy.wait()


def shards(x_panel, grad_out, row_state, col_state):
    vmem = pl.BlockSpec(memory_space=pltpu.VMEM)
    anym = pl.BlockSpec(memory_space=pl.ANY)
    dma = pltpu.SemaphoreType.DMA
    grad, new_rows, new_cols, k = pl.pallas_call(
        kernel,
        out_shape=(
            jax.ShapeDtypeStruct((2, FB, HB), f32),
            jax.ShapeDtypeStruct((2, FB), f32),
            jax.ShapeDtypeStruct((2, HB), f32),
            jax.ShapeDtypeStruct((1, 128), f32),
        ),
        in_specs=[anym, anym, vmem, vmem],
        out_specs=(anym, vmem, vmem, vmem),
        scratch_shapes=[
            pltpu.VMEM((2, TB, HB), jnp.bfloat16),
            pltpu.VMEM((NZ, TB, W), jnp.bfloat16),
            pltpu.VMEM((NC, XB, FB), jnp.bfloat16),
            pltpu.VMEM((FB, W), f32),
            pltpu.VMEM((2, FB, HB), f32),
            pltpu.VMEM((NC, 1, 2 * FB), f32),
            pltpu.VMEM((NZ, 1, 768), f32),
            pltpu.VMEM((NZ, 1, 896), f32),
            pltpu.VMEM((NC, 1, 128), f32),
            dma((4,)),
            dma((NZ, CH)),
            dma((NZ, CH)),
            dma((NZ, CH)),
            dma((NC,)),
            dma((NC,)),
            dma((NC,)),
            dma((NC,)),
            dma((NZ,)),
            dma((NZ,)),
            dma((NZ,)),
            dma((NZ,)),
            dma((NC,)),
            dma((NC,)),
        ],
        compiler_params=pltpu.CompilerParams(
            collective_id=0, has_side_effects=True, vmem_limit_bytes=56 * 1024 * 1024
        ),
        cost_estimate=pl.CostEstimate(
            flops=2 * D // NZ * W * 8192, bytes_accessed=3_000_000, transcendentals=0
        ),
    )(x_panel, grad_out, row_state, col_state)
    scale = k[0, :2]
    direction = (
        grad
        * (lax.rsqrt(new_rows) * scale[:, None])[:, :, None]
        * lax.rsqrt(new_cols)[:, None, :]
    )
    return (direction, new_rows, new_cols)


def solution(mesh):
    return jax.shard_map(
        shards,
        mesh=mesh,
        in_specs=(P("col", "row"), P(None, "row", "col"), P(None, "row"), P(None, "col")),
        out_specs=(P(None, "row", "col"), P(None, "row"), P(None, "col")),
        check_vma=False,
    )
```

time: 415 us -> 170 us (0.41)
  waiting for transfers between devices: 199 us -> 0 us
  blocking collectives: 193 us -> 0 us
  Pallas kernels: 0 us -> 162 us
  between operations: 14.1 us -> 0.67 us
  matrix products: 7 us -> 0 us
  local copies, waits for them, and re-layouts: 0.02 us -> 5.71 us
    all_gather x2 -> x0, waiting for transfers between devices: 198 us -> none  [the longest x1 128 us: shards(): lax.all_gather(grad_out, 'row', axis=1, tiled=True)]
    psum x3 -> x0, blocking collectives: 193 us -> none  [the longest x1 109 us: shards(): lax.psum(jnp.sum(update * update, axis=(1, 2)), ('row', 'col'))]
    pallas_call x0 -> x1, Pallas kernels: none -> 162 us  [shards(): pl.pallas_call(kernel, out_shape=(jax.ShapeDtypeStruct((2, FB, HB), f32),...]
    dot_general x1 -> x0, matrix products: 7 us -> none  [shards(): jnp.einsum('tr,mtc->mrc', x_whole, lax.all_gather(grad_out, 'row', axis=1...]
    unnamed x8 -> x10, local copies, waits for them, and re-layouts: 0.02 us -> 5.7 us
  transfers between devices with their start and end apart: 2 -> 0, of which waited for: 2 -> 0; matrix products, arithmetic and copies ran while one was open for 0% -> 0% of each run, Pallas kernels for 0% -> 0%
where the time goes in v1:
time: 170 us
  Pallas kernels  162 us (95%)
  local copies, waits for them, and re-layouts  5.71 us (3%)
    pallas_call x1, Pallas kernels, shards(): pl.pallas_call(kernel, out_shape=(jax.ShapeDtypeStruct((2, FB, HB), f32),...  162 us
    unnamed x10, local copies, waits for them, and re-layouts  5.7 us

profile of v1, /device:TPU:1, one launch (start us, length us, event | category | flops | bytes accessed | tf_op | source)
XLA Modules:
  0.0 170.2 jit_solution(5723030417105164032)
XLA Ops:
  0.6 2.3 %copy.7.g_hbm = bf16[2,512,320]{2,1,0:T(8,128)(2,1)} copy(bf16[2,512,320]{1,2,0:T(8,128)(2,1)} %param.5) | data formatting | bytes 1310720 | tf_op args[1]
  2.9 162.4 %shard_map.67 = (f32[2,256,320]{2,1,0:T(8,128)}, f32[2,256]{1,0:T(2,128)}, f32[2,320]{1,0:T(2,128)}, f32[1,128]{1,0:T(1,128)}) custom-call(bf16[256,256]{1,0:T(8,128)(2,1)} %x_hbm.1, bf16[2,512,320]{2,1,0:T(8,128)(2,1)} %copy.7.g_hbm, f32[2,256]{1,0:T(2,128)} %rs_ref.1, f32[2,320]{1,0:T(2,128)} %cs_ref.1), custom_call_target="tpu_custom_call" | custom-call | flops 2684354560 | bytes 3000000 | tf_op jit(solution)/shard_map/pallas_call | solution.py:312
  165.3 0.0 copy-start.2
  165.3 0.0 copy-start.1
  165.3 0.6 copy-done.2
  165.9 0.0 copy-start
  166.0 0.1 copy-done.1
  166.0 0.1 rsqrt_multiply_fusion
  166.1 0.5 copy-done
  166.6 1.3 multiply_multiply_fusion
  167.9 1.1 copy.8
  169.0 0.6 copy.11
  169.6 0.6 copy.12
  (2 shorter events, 0.0 us)
Async XLA Ops:
  165.3 0.6 copy-start.2
  165.3 0.7 copy-start.1
  165.9 0.7 copy-start

commit v2 on v0

v2 whole, which is shorter than its diff:
```python
import jax
import jax.numpy as jnp
from jax import lax
from jax.experimental import pallas as pl
from jax.experimental.pallas import tpu as pltpu
from jax.sharding import PartitionSpec as P

D = 4096
FF = 10240
NZ = 16
NC = 32
NY = 4
NX = 4
TB = 512
XB = 256
FB = 256
HB = 320
W = 2 * HB
CH = 4
RP = W // CH
TAIL = True

MESH = pl.DeviceIdType.MESH
f32 = jnp.float32

Z_ORDER = sorted(range(1, NZ), key=lambda k: -min(k, NZ - k))
C_ORDER = sorted(
    range(1, NC),
    key=lambda k: -(min(k // 8, 4 - k // 8) + min(k // 2 % 4, 4 - k // 2 % 4)),
)


def kernel(
    x_hbm, g_hbm, rs_ref, cs_ref,
    upd_hbm, nr_ref, nc_ref, k_ref,
    gbuf, xbuf, acc, csv, rowx, colx, ux, s3x,
    lsem, grecv, gright, gleft, xsend, xrecv, esend, erecv,
):
    z = lax.axis_index("row")
    c = lax.axis_index("col")
    core = lax.rem(c, 2)
    chip = c // 2
    x = lax.rem(chip, NX)
    y = chip // NX
    right = lax.rem(z + 1, NZ)
    left = lax.rem(z + NZ - 1, NZ)

    def at(yy, xx, cc):
        return (z, (yy * NX + xx) * 2 + cc)

    xp, xm = lax.rem(x + 1, NX), lax.rem(x + NX - 1, NX)
    yp, ym = lax.rem(y + 1, NY), lax.rem(y + NY - 1, NY)
    half = pl.ds(core * XB, XB)

    gcopy = pltpu.make_async_copy(g_hbm, gbuf.at[z], lsem.at[0])
    xcopy = pltpu.make_async_copy(x_hbm, xbuf.at[chip, half, :], lsem.at[1])
    gcopy.start()
    xcopy.start()

    near = [
        (right, c), (left, c),
        at(y, xp, core), at(y, xm, core), at(yp, x, core), at(ym, x, core),
        at(y, x, 1 - core),
    ]
    barrier = pltpu.get_barrier_semaphore()
    for dev in near:
        pl.semaphore_signal(barrier, inc=1, device_id=dev, device_id_type=MESH)
    pl.semaphore_wait(barrier, len(near))

    def hop(b, p, to_right):
        sems = gright if to_right else gleft
        part = gbuf.at[b, pl.ds(p * RP, RP), :]
        return pltpu.make_async_remote_copy(
            src_ref=part,
            dst_ref=part,
            send_sem=sems.at[b, p],
            recv_sem=grecv.at[b, p],
            device_id=(right if to_right else left, c),
            device_id_type=MESH,
        )

    gcopy.wait()
    for p in range(CH):
        hop(z, p, True).start()
        hop(z, p, False).start()

    def xmove(i, first, count, half, dev):
        ref = xbuf.at[pl.ds(first, count), half, :]
        return pltpu.make_async_remote_copy(
            src_ref=ref, dst_ref=ref, send_sem=xsend.at[i], recv_sem=xrecv.at[i],
            device_id=dev, device_id_type=MESH,
        )

    xx2 = lax.rem(x + 2, NX)
    yy2 = lax.rem(y + 2, NY)
    to_xp, to_xm = at(y, xp, core), at(y, xm, core)
    to_yp, to_ym = at(yp, x, core), at(ym, x, core)
    row0 = y * NX
    outgoing = [
        xmove(0, chip, 1, half, to_xp),
        xmove(1, chip, 1, half, to_xm),
        xmove(2, row0 + xm, 1, half, to_xp),
        xmove(3, row0, NX, half, to_yp),
        xmove(4, row0, NX, half, to_ym),
        xmove(5, ym * NX, NX // 2, half, to_yp),
        xmove(6, yp * NX + NX // 2, NX // 2, half, to_ym),
        xmove(7, 0, NX * NY, half, at(y, x, 1 - core)),
    ]
    other = pl.ds((1 - core) * XB, XB)
    incoming = [
        xmove(0, row0 + xm, 1, half, to_xp),
        xmove(1, row0 + xp, 1, half, to_xm),
        xmove(2, row0 + xx2, 1, half, to_xp),
        xmove(3, ym * NX, NX, half, to_yp),
        xmove(4, yp * NX, NX, half, to_ym),
        xmove(5, yy2 * NX, NX // 2, half, to_yp),
        xmove(6, yy2 * NX + NX // 2, NX // 2, half, to_ym),
        xmove(7, 0, NX * NY, other, at(y, x, 1 - core)),
    ]
    x_rounds = [((0, 1), (2,)), ((2,), (3, 4)), ((3, 4), (5, 6)), ((5, 6), (7,)), ((7,), ())]

    xcopy.wait()
    outgoing[0].start()
    outgoing[1].start()

    acc[...] = jnp.zeros_like(acc)
    csv[:, :HB] = cs_ref[0:1, :]
    csv[:, HB:] = cs_ref[1:2, :]

    def mm(b):
        acc[...] += jnp.dot(gbuf[b], xbuf[b], preferred_element_type=f32)

    def mm_piece(b, p):
        rows = pl.ds(p * RP, RP)
        acc[rows, :] += jnp.dot(gbuf[b, rows, :], xbuf[b], preferred_element_type=f32)

    def from_left(s):
        return lax.rem(z + NZ - s, NZ)

    def from_right(s):
        return lax.rem(z + s, NZ)

    @pl.loop(1, 7)
    def _(s):
        bl, br = from_left(s), from_right(s)
        for p in range(CH):
            hop(bl, p, True).wait_recv()
            hop(bl, p, True).start()
            hop(br, p, False).wait_recv()
            hop(br, p, False).start()
        for i, (arrived, leaving) in enumerate(x_rounds):
            @pl.when(s == i + 1)
            def _():
                for j in arrived:
                    incoming[j].wait_recv()
                for j in leaving:
                    outgoing[j].start()

    mm(z)

    @pl.loop(1, 4)
    def _(q):
        mm(from_left(q))
        mm(from_right(q))

    bl, br = from_left(7), from_right(7)
    for p in range(CH):
        hop(bl, p, True).wait_recv()
        if p < CH // 2:
            hop(bl, p, True).start()
        hop(br, p, False).wait_recv()
        if p >= CH // 2:
            hop(br, p, False).start()
        if p < CH - 1:
            mm(from_left(4 + p))
            mm(from_right(4 + p))
    mm(bl)
    mm(br)

    far = from_right(8)
    for p in range(CH // 2):
        for pp, to_right in ((p, True), (p + CH // 2, False)):
            hop(far, pp, to_right).wait_recv()
            mm_piece(far, pp)

    def partner(k, along_row):
        if along_row:
            return (lax.rem(z + k, NZ), c)
        dy, dx, dc = k // 8, k // 2 % 4, k % 2
        return at(
            lax.rem(y + dy, NY), lax.rem(x + dx, NX), 1 - core if dc else core
        )

    def send_all(i, buf, along_row):
        for k in Z_ORDER if along_row else C_ORDER:
            pltpu.make_async_remote_copy(
                src_ref=buf.at[0], dst_ref=buf.at[k],
                send_sem=esend.at[i], recv_sem=erecv.at[i],
                device_id=partner(k, along_row), device_id_type=MESH,
            ).start()

    def whole(i, buf, along_row):
        ref = buf.at[pl.ds(1, (NZ if along_row else NC) - 1)]
        return pltpu.make_async_remote_copy(
            src_ref=ref, dst_ref=ref,
            send_sem=esend.at[i], recv_sem=erecv.at[i],
            device_id=partner(1, along_row), device_id_type=MESH,
        )

    for m in range(2):
        gm = acc[m * HB : (m + 1) * HB, :]
        rowx[0, :, m * FB : (m + 1) * FB] = jnp.sum(
            gm * gm + 1e-30, axis=0, keepdims=True
        )
    send_all(0, rowx, False)

    def over_features(v):
        folded = v[:, :128] + v[:, 128:]
        return jnp.sum(folded.T, axis=0, keepdims=True)

    a = acc[...]
    colx[0] = over_features(a * a + 1e-30)
    send_all(1, colx, True)

    for j in range(8):
        outgoing[j].wait_send()

    @pl.loop(0, 7)
    def _(s):
        bl, br = from_left(s), from_right(s)
        for p in range(CH):
            hop(bl, p, True).wait_send()
            hop(br, p, False).wait_send()

    for p in range(CH // 2):
        hop(bl, p, True).wait_send()
        hop(br, p + CH // 2, False).wait_send()

    whole(0, rowx, False).wait_recv()
    row_tot = jnp.sum(rowx[...], axis=0)
    nr = []
    lane = lax.broadcasted_iota(jnp.int32, (1, 128), 1)
    for m in range(2):
        v = 0.7 * rs_ref[m : m + 1, :] + 0.3 * (row_tot[:, m * FB : (m + 1) * FB] / FF)
        nr_ref[m : m + 1, :] = v
        nr.append(v)
    hid = lax.broadcasted_iota(jnp.int32, (W, FB), 0)
    u = acc[...] * jnp.where(hid < HB, lax.rsqrt(nr[0]), lax.rsqrt(nr[1]))
    ux[0, :, 0:W] = over_features(u * u)
    ux[0, :, W : W + 128] = jnp.where(
        lane == 0,
        jnp.sum(nr[0], axis=1, keepdims=True),
        jnp.sum(nr[1], axis=1, keepdims=True),
    )
    send_all(2, ux, True)
    acc[...] = u

    whole(1, colx, True).wait_recv()
    col_tot = jnp.sum(colx[...], axis=0)
    ncv = 0.7 * csv[...] + 0.3 * (col_tot / D)
    nc_ref[0:1, :] = ncv[:, :HB]
    nc_ref[1:2, :] = ncv[:, HB:]
    ccol = jnp.broadcast_to(lax.rsqrt(ncv), (128, W)).T
    acc[:, :128] = acc[:, :128] * ccol
    acc[:, 128:] = acc[:, 128:] * ccol
    ucopy = pltpu.make_async_copy(acc, upd_hbm, lsem.at[2])
    ucopy.start()

    whole(2, ux, True).wait_recv()
    u_tot = jnp.sum(ux[...], axis=0)
    share = u_tot[:, 0:W] / ncv
    first = lax.broadcasted_iota(jnp.int32, (1, W), 1) < HB
    s3x[0] = jnp.where(
        lane == 0,
        jnp.sum(jnp.where(first, share, 0.0), axis=1, keepdims=True),
        jnp.sum(jnp.where(first, 0.0, share), axis=1, keepdims=True),
    )
    send_all(3, s3x, False)
    level = u_tot[:, W : W + 128] / D
    whole(0, rowx, False).wait_send()
    whole(1, colx, True).wait_send()
    whole(2, ux, True).wait_send()
    ucopy.wait()
    whole(3, s3x, False).wait_recv()
    s_tot = jnp.sum(s3x[...], axis=0)
    urms = jnp.sqrt(level * (s_tot / (D * FF)))
    k_ref[...] = jnp.sqrt(level) / jnp.maximum(1.0, urms)
    whole(3, s3x, False).wait_send()


def finish(upd_ref, nr_in, nc_in, k_ref, out_ref, nr_ref, nc_ref):
    m = pl.program_id(0)
    k = k_ref[...]
    out_ref[...] = upd_ref[...] * jnp.where(m == 0, k[:, 0:1], k[:, 1:2])

    @pl.when(m == 0)
    def _():
        nr_ref[...] = nr_in[...]
        nc_ref[...] = nc_in[...]


def shards(x_panel, grad_out, row_state, col_state):
    vmem = pl.BlockSpec(memory_space=pltpu.VMEM)
    anym = pl.BlockSpec(memory_space=pl.ANY)
    dma = pltpu.SemaphoreType.DMA
    grad_t = jnp.swapaxes(grad_out, 1, 2).reshape(W, TB)
    upd, new_rows, new_cols, k = pl.pallas_call(
        kernel,
        out_shape=(
            jax.ShapeDtypeStruct((W, FB), f32),
            jax.ShapeDtypeStruct((2, FB), f32),
            jax.ShapeDtypeStruct((2, HB), f32),
            jax.ShapeDtypeStruct((1, 128), f32),
        ),
        in_specs=[anym, anym, vmem, vmem],
        out_specs=(anym, vmem, vmem, vmem),
        scratch_shapes=[
            pltpu.VMEM((NZ, W, TB), jnp.bfloat16),
            pltpu.VMEM((NZ, TB, FB), jnp.bfloat16),
            pltpu.VMEM((W, FB), f32),
            pltpu.VMEM((1, W), f32),
            pltpu.VMEM((NC, 1, 2 * FB), f32),
            pltpu.VMEM((NZ, 1, W), f32),
            pltpu.VMEM((NZ, 1, W + 128), f32),
            pltpu.VMEM((NC, 1, 128), f32),
            dma((3,)),
            dma((NZ, CH)),
            dma((NZ, CH)),
            dma((NZ, CH)),
            dma((8,)),
            dma((8,)),
            dma((4,)),
            dma((4,)),
        ],
        compiler_params=pltpu.CompilerParams(
            collective_id=0, has_side_effects=True, vmem_limit_bytes=56 * 1024 * 1024
        ),
        cost_estimate=pl.CostEstimate(
            flops=2 * FB * W * 8192, bytes_accessed=3_000_000, transcendentals=0
        ),
    )(x_panel, grad_t, row_state, col_state)
    half = pl.BlockSpec((HB, FB), lambda m: (m, 0))
    direction, new_rows, new_cols = pl.pallas_call(
        finish,
        grid=(2,),
        out_shape=(
            jax.ShapeDtypeStruct((W, FB), f32),
            jax.ShapeDtypeStruct((2, FB), f32),
            jax.ShapeDtypeStruct((2, HB), f32),
        ),
        in_specs=[half, vmem, vmem, vmem],
        out_specs=(half, vmem, vmem),
    )(upd, new_rows, new_cols, k)
    direction = jnp.swapaxes(direction.reshape(2, HB, FB), 1, 2)
    return (direction, new_rows, new_cols)


def solution(mesh):
    return jax.shard_map(
        shards,
        mesh=mesh,
        in_specs=(P("col", "row"), P(None, "row", "col"), P(None, "row"), P(None, "col")),
        out_specs=(P(None, "row", "col"), P(None, "row"), P(None, "col")),
        check_vma=False,
    )
```

time: 415 us -> 144 us (0.35)
  waiting for transfers between devices: 199 us -> 0 us
  blocking collectives: 193 us -> 0 us
  Pallas kernels: 0 us -> 143 us
  between operations: 14.1 us -> 0.64 us
  matrix products: 7 us -> 0 us
    all_gather x2 -> x0, waiting for transfers between devices: 198 us -> none  [the longest x1 128 us: shards(): lax.all_gather(grad_out, 'row', axis=1, tiled=True)]
    psum x3 -> x0, blocking collectives: 193 us -> none  [the longest x1 109 us: shards(): lax.psum(jnp.sum(update * update, axis=(1, 2)), ('row', 'col'))]
    pallas_call x0 -> x2, Pallas kernels: none -> 143 us  [the longest x1 141 us: shards(): pl.pallas_call(kernel, out_shape=(jax.ShapeDtypeStruct((W, FB), f32), jax...]
    dot_general x1 -> x0, matrix products: 7 us -> none  [shards(): jnp.einsum('tr,mtc->mrc', x_whole, lax.all_gather(grad_out, 'row', axis=1...]
  transfers between devices with their start and end apart: 2 -> 0, of which waited for: 2 -> 0; matrix products, arithmetic and copies ran while one was open for 0% -> 0% of each run, Pallas kernels for 0% -> 0%
where the time goes in v2:
time: 144 us
  Pallas kernels  143 us (99%)
    pallas_call x1, Pallas kernels, shards(): pl.pallas_call(kernel, out_shape=(jax.ShapeDtypeStruct((W, FB), f32), jax...  141 us

profile of v2, /device:TPU:1, one launch (start us, length us, event | category | flops | bytes accessed | tf_op | source)
XLA Modules:
  0.0 144.0 jit_solution(7456506504294282432)
XLA Ops:
  0.6 141.2 %shard_map.67 = (f32[640,256]{1,0:T(8,128)}, f32[2,256]{1,0:T(2,128)}, f32[2,320]{1,0:T(2,128)}, f32[1,128]{1,0:T(1,128)}) custom-call(bf16[256,256]{1,0:T(8,128)(2,1)} %x_hbm.1, bf16[640,512]{1,0:T(8,128)(2,1)} %bitcast.6, f32[2,256]{1,0:T(2,128)} %rs_ref.1, f32[2,320]{1,0:T(2,128)} %cs_ref.1), custom_call_target="tpu_custom_call" | custom-call | flops 2684354560 | bytes 3000000 | tf_op jit(solution)/shard_map/pallas_call | solution.py:307
  141.9 2.1 %shard_map.68 = (f32[640,256]{1,0:T(8,128)}, f32[2,256]{1,0:T(2,128)}, f32[2,320]{1,0:T(2,128)}) custom-call(f32[640,256]{1,0:T(8,128)} %get-tuple-element.10.upd_ref, f32[2,256]{1,0:T(2,128)} %get-tuple-element.11.nr_in, f32[2,320]{1,0:T(2,128)} %get-tuple-element.12.nc_in, f32[1,128]{1,0:T(1,128)} %get-tuple-element.13.k_ref), custom_call_target="tpu_custom_call" | custom-call | tf_op jit(solution)/shard_map/pallas_call | solution.py:343

commit v3 on v2

--- a/solution.py
+++ b/solution.py
@@ -16,9 +16,10 @@
 FB = 256
 HB = 320
 W = 2 * HB
-CH = 4
+CH = 2
 RP = W // CH
-TAIL = True
+QS = 4
+QP = W // QS
 
 MESH = pl.DeviceIdType.MESH
 f32 = jnp.float32
@@ -54,9 +55,6 @@
 
     gcopy = pltpu.make_async_copy(g_hbm, gbuf.at[z], lsem.at[0])
     xcopy = pltpu.make_async_copy(x_hbm, xbuf.at[chip, half, :], lsem.at[1])
-    gcopy.start()
-    xcopy.start()
-
     near = [
         (right, c), (left, c),
         at(y, xp, core), at(y, xm, core), at(yp, x, core), at(ym, x, core),
@@ -65,13 +63,15 @@
     barrier = pltpu.get_barrier_semaphore()
     for dev in near:
         pl.semaphore_signal(barrier, inc=1, device_id=dev, device_id_type=MESH)
+    gcopy.start()
+    xcopy.start()
     pl.semaphore_wait(barrier, len(near))
 
-    def hop(b, p, to_right):
+    def hop(b, p, to_right, own=False):
         sems = gright if to_right else gleft
         part = gbuf.at[b, pl.ds(p * RP, RP), :]
         return pltpu.make_async_remote_copy(
-            src_ref=part,
+            src_ref=g_hbm.at[pl.ds(p * RP, RP), :] if own else part,
             dst_ref=part,
             send_sem=sems.at[b, p],
             recv_sem=grecv.at[b, p],
@@ -79,10 +79,9 @@
             device_id_type=MESH,
         )
 
-    gcopy.wait()
     for p in range(CH):
-        hop(z, p, True).start()
-        hop(z, p, False).start()
+        hop(z, p, True, own=True).start()
+        hop(z, p, False, own=True).start()
 
     def xmove(i, first, count, half, dev):
         ref = xbuf.at[pl.ds(first, count), half, :]
@@ -156,6 +155,7 @@
                 for j in leaving:
                     outgoing[j].start()
 
+    gcopy.wait()
     mm(z)
 
     @pl.loop(1, 4)
@@ -171,17 +171,22 @@
         hop(br, p, False).wait_recv()
         if p >= CH // 2:
             hop(br, p, False).start()
-        if p < CH - 1:
-            mm(from_left(4 + p))
-            mm(from_right(4 + p))
-    mm(bl)
-    mm(br)
+        if p == 0:
+            for q in (4, 5):
+                mm(from_left(q))
+                mm(from_right(q))
+    for q in (6, 7):
+        mm(from_left(q))
+        mm(from_right(q))
 
     far = from_right(8)
-    for p in range(CH // 2):
-        for pp, to_right in ((p, True), (p + CH // 2, False)):
-            hop(far, pp, to_right).wait_recv()
-            mm_piece(far, pp)
+    for m, to_right in ((0, True), (1, False)):
+        hop(far, m, to_right).wait_recv()
+        mm_piece(far, m)
+        gm = acc[m * HB : (m + 1) * HB, :]
+        rowx[0, :, m * FB : (m + 1) * FB] = jnp.sum(
+            gm * gm + 1e-30, axis=0, keepdims=True
+        )
 
     def partner(k, along_row):
         if along_row:
@@ -207,11 +212,6 @@
             device_id=partner(1, along_row), device_id_type=MESH,
         )
 
-    for m in range(2):
-        gm = acc[m * HB : (m + 1) * HB, :]
-        rowx[0, :, m * FB : (m + 1) * FB] = jnp.sum(
-            gm * gm + 1e-30, axis=0, keepdims=True
-        )
     send_all(0, rowx, False)
 
     def over_features(v):
@@ -225,7 +225,11 @@
     for j in range(8):
         outgoing[j].wait_send()
 
-    @pl.loop(0, 7)
+    for p in range(CH):
+        hop(z, p, True, own=True).wait_send()
+        hop(z, p, False, own=True).wait_send()
+
+    @pl.loop(1, 7)
     def _(s):
         bl, br = from_left(s), from_right(s)
         for p in range(CH):
@@ -288,15 +292,34 @@
     whole(3, s3x, False).wait_send()
 
 
-def finish(upd_ref, nr_in, nc_in, k_ref, out_ref, nr_ref, nc_ref):
-    m = pl.program_id(0)
-    k = k_ref[...]
-    out_ref[...] = upd_ref[...] * jnp.where(m == 0, k[:, 0:1], k[:, 1:2])
-
-    @pl.when(m == 0)
-    def _():
-        nr_ref[...] = nr_in[...]
-        nc_ref[...] = nc_in[...]
+def finish(
+    upd_hbm, nr_hbm, nc_hbm, k_hbm, out_hbm, nr_out, nc_out,
+    buf, nr, nc, k, in_sem, out_sem,
+):
+    def piece(ref, i):
+        return ref.at[pl.ds(i * QP, QP), :]
+
+    copy = pltpu.make_async_copy
+    ins = [copy(k_hbm, k, in_sem.at[QS])]
+    ins += [copy(piece(upd_hbm, i), piece(buf, i), in_sem.at[i]) for i in range(QS)]
+    small = [copy(nr_hbm, nr, in_sem.at[QS + 1]), copy(nc_hbm, nc, in_sem.at[QS + 2])]
+    for cp in ins + small:
+        cp.start()
+    outs = [copy(piece(buf, i), piece(out_hbm, i), out_sem.at[i]) for i in range(QS)]
+    outs += [copy(nr, nr_out, out_sem.at[QS]), copy(nc, nc_out, out_sem.at[QS + 1])]
+    ins[0].wait()
+    scale = k[...]
+    for i in range(QS):
+        ins[1 + i].wait()
+        m = i // (QS // 2)
+        rows = pl.ds(i * QP, QP)
+        buf[rows, :] = buf[rows, :] * scale[:, m : m + 1]
+        outs[i].start()
+    for cp, out in zip(small, outs[QS:]):
+        cp.wait()
+        out.start()
+    for out in outs:
+        out.wait()
 
 
 def shards(x_panel, grad_out, row_state, col_state):
@@ -339,17 +362,23 @@
             flops=2 * FB * W * 8192, bytes_accessed=3_000_000, transcendentals=0
         ),
     )(x_panel, grad_t, row_state, col_state)
-    half = pl.BlockSpec((HB, FB), lambda m: (m, 0))
     direction, new_rows, new_cols = pl.pallas_call(
         finish,
-        grid=(2,),
         out_shape=(
             jax.ShapeDtypeStruct((W, FB), f32),
             jax.ShapeDtypeStruct((2, FB), f32),
             jax.ShapeDtypeStruct((2, HB), f32),
         ),
-        in_specs=[half, vmem, vmem, vmem],
-        out_specs=(half, vmem, vmem),
+        in_specs=[anym, anym, anym, anym],
+        out_specs=(anym, anym, anym),
+        scratch_shapes=[
+            pltpu.VMEM((W, FB), f32),
+            pltpu.VMEM((2, FB), f32),
+            pltpu.VMEM((2, HB), f32),
+            pltpu.VMEM((1, 128), f32),
+            dma((QS + 3,)),
+            dma((QS + 2,)),
+        ],
     )(upd, new_rows, new_cols, k)
     direction = jnp.swapaxes(direction.reshape(2, HB, FB), 1, 2)
     return (direction, new_rows, new_cols)

time: 144 us -> 144 us (level)
  no operation moved by 1% of the time
where the time goes in v3:
time: 144 us
  Pallas kernels  143 us (99%)
    pallas_call x1, Pallas kernels, shards(): pl.pallas_call(kernel, out_shape=(jax.ShapeDtypeStruct((W, FB), f32), jax...  141 us

profile of v3, /device:TPU:1, one launch (start us, length us, event | category | flops | bytes accessed | tf_op | source)
XLA Modules:
  0.0 143.8 jit_solution(474987916159716700)
XLA Ops:
  0.6 141.2 %shard_map.67 = (f32[640,256]{1,0:T(8,128)}, f32[2,256]{1,0:T(2,128)}, f32[2,320]{1,0:T(2,128)}, f32[1,128]{1,0:T(1,128)}) custom-call(bf16[256,256]{1,0:T(8,128)(2,1)} %x_hbm.1, bf16[640,512]{1,0:T(8,128)(2,1)} %bitcast.6, f32[2,256]{1,0:T(2,128)} %rs_ref.1, f32[2,320]{1,0:T(2,128)} %cs_ref.1), custom_call_target="tpu_custom_call" | custom-call | flops 2684354560 | bytes 3000000 | tf_op jit(solution)/shard_map/pallas_call | solution.py:330
  141.8 2.0 %shard_map.68 = (f32[640,256]{1,0:T(8,128)}, f32[2,256]{1,0:T(2,128)}, f32[2,320]{1,0:T(2,128)}) custom-call(f32[640,256]{1,0:T(8,128)} %get-tuple-element.10.upd_hbm, f32[2,256]{1,0:T(2,128)} %get-tuple-element.11.nr_hbm, f32[2,320]{1,0:T(2,128)} %get-tuple-element.12.nc_hbm, f32[1,128]{1,0:T(1,128)} %get-tuple-element.13.k_hbm), custom_call_target="tpu_custom_call" | custom-call | tf_op jit(solution)/shard_map/pallas_call | solution.py:365

commit v4 on v3

--- a/solution.py
+++ b/solution.py
@@ -81,7 +81,7 @@
 
     for p in range(CH):
         hop(z, p, True, own=True).start()
-        hop(z, p, False, own=True).start()
+        hop(z, CH - 1 - p, False, own=True).start()
 
     def xmove(i, first, count, half, dev):
         ref = xbuf.at[pl.ds(first, count), half, :]
@@ -145,8 +145,8 @@
         for p in range(CH):
             hop(bl, p, True).wait_recv()
             hop(bl, p, True).start()
-            hop(br, p, False).wait_recv()
-            hop(br, p, False).start()
+            hop(br, CH - 1 - p, False).wait_recv()
+            hop(br, CH - 1 - p, False).start()
         for i, (arrived, leaving) in enumerate(x_rounds):
             @pl.when(s == i + 1)
             def _():
@@ -168,9 +168,9 @@
         hop(bl, p, True).wait_recv()
         if p < CH // 2:
             hop(bl, p, True).start()
-        hop(br, p, False).wait_recv()
-        if p >= CH // 2:
-            hop(br, p, False).start()
+        hop(br, CH - 1 - p, False).wait_recv()
+        if p < CH // 2:
+            hop(br, CH - 1 - p, False).start()
         if p == 0:
             for q in (4, 5):
                 mm(from_left(q))

time: 144 us -> 143 us (level)
  no operation moved by 1% of the time
where the time goes in v4:
time: 143 us
  Pallas kernels  143 us (100%)
    pallas_call x1, Pallas kernels, shards(): pl.pallas_call(kernel, out_shape=(jax.ShapeDtypeStruct((W, FB), f32), jax...  141 us

profile of v4, /device:TPU:1, one launch (start us, length us, event | category | flops | bytes accessed | tf_op | source)
XLA Modules:
  0.0 143.3 jit_solution(13822976599840866277)
XLA Ops:
  0.6 140.7 %shard_map.67 = (f32[640,256]{1,0:T(8,128)}, f32[2,256]{1,0:T(2,128)}, f32[2,320]{1,0:T(2,128)}, f32[1,128]{1,0:T(1,128)}) custom-call(bf16[256,256]{1,0:T(8,128)(2,1)} %x_hbm.1, bf16[640,512]{1,0:T(8,128)(2,1)} %bitcast.6, f32[2,256]{1,0:T(2,128)} %rs_ref.1, f32[2,320]{1,0:T(2,128)} %cs_ref.1), custom_call_target="tpu_custom_call" | custom-call | flops 2684354560 | bytes 3000000 | tf_op jit(solution)/shard_map/pallas_call | solution.py:330
  141.3 2.0 %shard_map.68 = (f32[640,256]{1,0:T(8,128)}, f32[2,256]{1,0:T(2,128)}, f32[2,320]{1,0:T(2,128)}) custom-call(f32[640,256]{1,0:T(8,128)} %get-tuple-element.10.upd_hbm, f32[2,256]{1,0:T(2,128)} %get-tuple-element.11.nr_hbm, f32[2,320]{1,0:T(2,128)} %get-tuple-element.12.nc_hbm, f32[1,128]{1,0:T(1,128)} %get-tuple-element.13.k_hbm), custom_call_target="tpu_custom_call" | custom-call | tf_op jit(solution)/shard_map/pallas_call | solution.py:365
